TPU v7x, 128 devices: a whole 4x4x4 slice. The times are simulated.
128 devices in a mesh: latent: 16 (over x_hi, y, core), row: 4 (over z), group: 2 (over x_lo).
Axes of the slice: x: 4 (x_hi: 2, x_lo: 2; x = x_hi * 2 + x_lo), y: 4, z: 4, core: 2. Of those that a mesh axis runs over, the one named last changes fastest.
Arguments:
- attn_out: bfloat16 [512, 8192], P(None, ('latent', 'group')), may hold values from -6 to 6
- out_proj: bfloat16 [8192, 8192], P(('latent', 'group'), 'row'), may hold values from -0.0625 to 0.0625
- resid: bfloat16 [512, 8192], P(None, 'row'), may hold values from -6 to 6
- enc_weight: bfloat16 [8192, 65536], P('row', ('latent', 'group')), may hold values from -0.0625 to 0.0625
- enc_bias: float32 [65536], P(('latent', 'group')), may hold values from -1 to 0.5
- dec_bias: float32 [8192], P('row'), may hold values from -3 to 3
- moment: float32 [65536], P(('latent', 'group')), may hold values from 0.001953125 to 0.05859375
Outputs:
- update: bfloat16 [8192, 65536], P('row', ('latent', 'group'))
- new_moment: float32 [65536], P(('latent', 'group'))
All inputs are finite; a program needn't handle non-finite values.
Results may differ from a plain program's by a relative error of at most 0.012.
Values may be sent and summed in bfloat16 or wider, within the bound.
No kernel may reach another device: no remote copies, remote signals or barrier semaphores. Data moves between devices by JAX's collectives and lax.ppermute only.
A program may use at most 128 MiB of HBM per device.

v0:
```python
import jax
import jax.numpy as jnp
from jax import lax
from jax.sharding import PartitionSpec as P

D = 8192


SHARP = 4.0
SPARSITY = 2.0
BETA = 0.9


def contract_rows(left, right):
    return lax.dot_general(
        left, right, (((0,), (0,)), ((), ())), preferred_element_type=jnp.float32
    )


def contract_cols(left, right):
    return lax.dot_general(
        left, right, (((1,), (1,)), ((), ())), preferred_element_type=jnp.float32
    )


def body(attn_out, out_proj, resid, enc_weight, enc_bias, dec_bias, moment):
    tokens = attn_out.shape[0]
    projected = lax.psum(
        jnp.dot(attn_out, out_proj, preferred_element_type=jnp.float32), ("latent", "group")
    )
    harvested = (resid.astype(jnp.float32) + projected).astype(jnp.bfloat16)
    preact = (
        lax.psum(jnp.dot(harvested, enc_weight, preferred_element_type=jnp.float32), "row")
        + enc_bias
    )
    codes = (jax.nn.softplus(SHARP * preact) / SHARP).astype(jnp.bfloat16)
    slopes = jax.nn.sigmoid(SHARP * preact)
    recon = (
        lax.psum(contract_cols(codes, enc_weight).astype(jnp.bfloat16), ("latent", "group")).astype(
            jnp.float32
        )
        + dec_bias
    )
    recon_grad = ((recon - harvested.astype(jnp.float32)) / tokens).astype(jnp.bfloat16)
    feedback = (
        lax.psum(
            jnp.dot(recon_grad, enc_weight, preferred_element_type=jnp.float32).astype(
                jnp.bfloat16
            ),
            "row",
        ).astype(jnp.float32)
        + SPARSITY / tokens
    )
    code_grad = (feedback * slopes).astype(jnp.bfloat16)
    weight_grad = contract_rows(harvested, code_grad) + contract_rows(recon_grad, codes)
    energy = lax.psum(jnp.sum(weight_grad * weight_grad, axis=0), "row") / D
    fresh = BETA * moment + (1.0 - BETA) * energy
    update = (weight_grad / jnp.sqrt(fresh)).astype(jnp.bfloat16)
    return (update, fresh)


def solution(mesh):
    placed = (
        P(None, ("latent", "group")),
        P(("latent", "group"), "row"),
        P(None, "row"),
        P("row", ("latent", "group")),
        P(("latent", "group")),
        P("row"),
        P(("latent", "group")),
    )
    return jax.shard_map(
        body,
        mesh=mesh,
        in_specs=placed,
        out_specs=(P("row", ("latent", "group")), P(("latent", "group"))),
        check_vma=False,
    )
```

profile of v0, /device:TPU:0, one launch (start us, length us, event | category | flops | bytes accessed | tf_op | source)
XLA Modules:
  0.0 470.2 jit_solution(8662551406729444519)
XLA Ops:
  7.2 0.0 copy-start
  7.2 0.0 all-reduce.5.cloned.1.call-start
  7.2 1.2 copy-done
  8.4 3.7 fusion.15
  12.1 0.0 all-reduce.5.cloned.1.call-update
  12.1 0.0 all-reduce.7.cloned.1.call-start
  12.1 114.0 %all-reduce.5.cloned.1.call-done = f32[512,2048]{1,0:T(8,128)} async-done(((f32[512,2048]{1,0:T(8,128)}), f32[512,2048]{1,0:T(8,128)}) %all-reduce.5.cloned.1.call-update) | async-done | bytes 4194320 | tf_op jit(solution)/shard_map/psum | solution.py:28
  126.2 0.0 copy-start.7
  126.2 3.7 add_convert_fusion
  129.9 1.5 copy-done.7
  131.4 6.1 %fusion.16 = f32[512,2048]{1,0:T(8,128)} fusion(bf16[512,2048]{1,0:T(8,128)(2,1)S(1)} %add_convert_fusion, bf16[2048,2048]{1,0:T(8,128)(2,1)S(1)} %copy-done.7), kind=kOutput, calls=%fused_computation.25 | convolution fusion | flops 4294967296 | bytes 14680064 | tf_op jit(solution)/shard_map/dot_general | solution.py:33
  137.5 0.0 copy-start.6
  137.5 0.0 all-reduce.7.cloned.1.call-update
  137.6 0.0 copy-start.4
  137.6 0.0 all-reduce.9.cloned.1.call-start
  137.6 92.8 %all-reduce.7.cloned.1.call-done = f32[512,2048]{1,0:T(8,128)} async-done(((f32[512,2048]{1,0:T(8,128)}), f32[512,2048]{1,0:T(8,128)}) %all-reduce.7.cloned.1.call-update) | async-done | bytes 4194320 | tf_op jit(solution)/shard_map/psum | solution.py:33
  230.4 0.0 copy-done.6
  230.5 12.4 %convolution_convert_fusion.1 = bf16[512,2048]{1,0:T(8,128)(2,1)} fusion(bf16[2048,2048]{1,0:T(8,128)(2,1)} %param.10, f32[512,2048]{1,0:T(8,128)} %all-reduce.7.cloned.1.call-done, f32[2048]{0:T(1024)S(1)} %copy-done.6), kind=kOutput, calls=%fused_computation.11 | convolution fusion | flops 4306501632 | bytes 14688256 | tf_op jit(solution)/shard_map/dot_general | solution.py:21
  242.9 0.0 all-reduce.9.cloned.1.call-update
  242.9 0.2 all-reduce.11.cloned.1.call-start
  243.1 106.9 %all-reduce.9.cloned.1.call-done = bf16[512,2048]{1,0:T(8,128)(2,1)} async-done(((bf16[512,2048]{1,0:T(8,128)(2,1)}), bf16[512,2048]{1,0:T(8,128)(2,1)}) %all-reduce.9.cloned.1.call-update) | async-done | bytes 2097168 | tf_op jit(solution)/shard_map/psum | solution.py:39
  350.0 0.0 copy-done.4
  350.0 9.8 %convolution_convert_fusion = bf16[512,2048]{1,0:T(8,128)(2,1)} fusion(bf16[2048,2048]{1,0:T(8,128)(2,1)} %param.10, bf16[512,2048]{1,0:T(8,128)(2,1)S(1)} %add_convert_fusion, bf16[512,2048]{1,0:T(8,128)(2,1)} %all-reduce.9.cloned.1.call-done, f32[2048]{0:T(1024)S(1)} %copy-done.4), kind=kOutput, calls=%fused_computation.10 | convolution fusion | flops 4302307328 | bytes 14688256 | tf_op jit(solution)/shard_map/dot_general | solution.py:47
  359.9 0.0 all-reduce.11.cloned.1.call-update
  359.9 58.8 %all-reduce.11.cloned.1.call-done = bf16[512,2048]{1,0:T(8,128)(2,1)} async-done(((bf16[512,2048]{1,0:T(8,128)(2,1)}), bf16[512,2048]{1,0:T(8,128)(2,1)}) %all-reduce.11.cloned.1.call-update) | async-done | bytes 2097168 | tf_op jit(solution)/shard_map/psum | solution.py:46
  418.7 0.0 copy-start.2
  418.7 0.0 copy-start.3
  418.7 11.2 %fusion.2 = f32[2048,2048]{1,0:T(8,128)} fusion(bf16[512,2048]{1,0:T(8,128)(2,1)S(1)} %add_convert_fusion, bf16[512,2048]{1,0:T(8,128)(2,1)} %all-reduce.11.cloned.1.call-done, f32[512,2048]{1,0:T(8,128)} %all-reduce.7.cloned.1.call-done, f32[2048]{0:T(1024)S(1)} %copy-done.6), kind=kOutput, calls=%fused_computation.12 | convolution fusion | flops 4304404480 | bytes 25174016 | tf_op jit(solution)/shard_map/dot_general | solution.py:15
  430.0 0.0 copy-done.2
  430.0 0.0 copy-done.3
  430.0 0.0 copy-start.5
  430.0 14.8 %multiply_reduce_fusion = (f32[2048]{0:T(1024)S(1)}, f32[2048,2048]{1,0:T(8,128)}) fusion(f32[2048,2048]{1,0:T(8,128)} %fusion.2, f32[512,2048]{1,0:T(8,128)S(1)} %copy-done.3, f32[2048]{0:T(1024)S(1)} %copy-done.6, bf16[512,2048]{1,0:T(8,128)(2,1)S(1)} %add_convert_fusion, bf16[512,2048]{1,0:T(8,128)(2,1)S(1)} %copy-done.2, f32[2048]{0:T(1024)S(1)} %copy-done.4), kind=kOutput, calls=%fused_computation.1 | convolution fusion | flops 4324325376 | bytes 41967616 | tf_op jit(solution)/shard_map/dot_general | solution.py:15
  444.8 8.5 %psum.39 = f32[2048]{0:T(1024)S(1)} all-reduce(f32[2048]{0:T(1024)S(1)} %get-tuple-element.4), channel_id=1, replica_groups=mesh['latent'=16,'row'=4,'group'=2] {'row'}, use_global_device_ids=true, to_apply=%region_5.6 | all-reduce | flops 2048 | bytes 16384 | tf_op jit(solution)/shard_map/psum | solution.py:56
  453.4 0.0 copy-done.5
  453.4 0.6 fusion.14
  454.0 0.0 copy-start.1
  454.0 9.7 %divide_convert_fusion = bf16[2048,2048]{1,0:T(8,128)(2,1)} fusion(f32[2048,2048]{1,0:T(8,128)} %get-tuple-element.5, f32[2048]{0:T(1024)S(1)} %get-tuple-element.2), kind=kLoop, calls=%fused_computation | loop fusion | flops 8388608 | bytes 25174016 | tf_op jit(solution)/shard_map/convert_element_type | solution.py:58
  463.7 0.0 copy-done.1
Async XLA Ops:
  7.2 1.2 copy-start
  7.2 119.0 %all-reduce.5.cloned.1.call-start = ((), (), s32[]{:S(2)}) async-start(), calls=%async_computation | async-start | bytes 8388608 | tf_op jit(solution)/shard_map/psum | solution.py:28
  12.1 218.3 %all-reduce.7.cloned.1.call-start = ((), (), s32[]{:S(2)}) async-start(), calls=%async_computation.1 | async-start | bytes 8388608 | tf_op jit(solution)/shard_map/psum | solution.py:33
  126.2 5.2 %copy-start.7 = (bf16[2048,2048]{1,0:T(8,128)(2,1)S(1)}, bf16[2048,2048]{1,0:T(8,128)(2,1)}, u32[]{:S(2)}) copy-start(bf16[2048,2048]{1,0:T(8,128)(2,1)} %param.10) | copy-start | bytes 25165828
  137.5 92.9 %copy-start.6 = (f32[2048]{0:T(1024)S(1)}, f32[2048]{0:T(1024)}, u32[]{:S(2)}) copy-start(f32[2048]{0:T(1024)} %param.11) | copy-start | bytes 24580
  137.6 212.5 %copy-start.4 = (f32[2048]{0:T(1024)S(1)}, f32[2048]{0:T(1024)}, u32[]{:S(2)}) copy-start(f32[2048]{0:T(1024)} %param.12) | copy-start | bytes 24580
  137.6 212.4 %all-reduce.9.cloned.1.call-start = ((), (), s32[]{:S(2)}) async-start(), calls=%async_computation.2 | async-start | bytes 4194304 | tf_op jit(solution)/shard_map/psum | solution.py:39
  242.9 175.8 %all-reduce.11.cloned.1.call-start = ((), (), s32[]{:S(2)}) async-start(), calls=%async_computation.3 | async-start | bytes 4194304 | tf_op jit(solution)/shard_map/psum | solution.py:46
  418.7 11.3 %copy-start.2 = (bf16[512,2048]{1,0:T(8,128)(2,1)S(1)}, bf16[512,2048]{1,0:T(8,128)(2,1)}, u32[]{:S(2)}) copy-start(bf16[512,2048]{1,0:T(8,128)(2,1)} %all-reduce.9.cloned.1.call-done) | copy-start | bytes 6291460
  418.7 11.3 %copy-start.3 = (f32[512,2048]{1,0:T(8,128)S(1)}, f32[512,2048]{1,0:T(8,128)}, u32[]{:S(2)}) copy-start(f32[512,2048]{1,0:T(8,128)} %all-reduce.7.cloned.1.call-done) | copy-start | bytes 12582916
  430.0 23.4 %copy-start.5 = (f32[2048]{0:T(1024)S(1)}, f32[2048]{0:T(1024)}, u32[]{:S(2)}) copy-start(f32[2048]{0:T(1024)} %param.13) | copy-start | bytes 24580
  454.0 9.7 %copy-start.1 = (bf16[256,2048]{1,0:T(8,128)(2,1)S(1)}, bf16[256,2048]{1,0:T(8,128)(2,1)}, u32[]{:S(2)}) copy-start(bf16[256,2048]{1,0:T(8,128)(2,1)} %param.8) | copy-start | bytes 3145732
Sparse Core Ops, SparseCore 0:
  12.2 113.8 all-reduce.4
  137.7 92.7 all-reduce.6
  243.0 106.9 all-reduce.8
  360.0 58.6 all-reduce.10
where the time goes:
time: 470 us
  waiting for transfers between devices  373 us (79%)
  matrix products  58.1 us (12%)
  other arithmetic  14 us (3%)
  between operations  13.8 us (3%)
  blocking collectives  8.55 us (2%)
    psum x1, waiting for transfers between devices, body(): lax.psum(jnp.dot(attn_out, out_proj, preferred_element_type=jnp.float32),...  114 us
    psum x1, waiting for transfers between devices, body(): lax.psum(contract_cols(codes, enc_weight).astype(jnp.bfloat16), ('latent'...  107 us
    psum x1, waiting for transfers between devices, body(): lax.psum(jnp.dot(harvested, enc_weight, preferred_element_type=jnp.float3...  92.8 us
    psum x1, waiting for transfers between devices, body(): lax.psum(jnp.dot(recon_grad, enc_weight, preferred_element_type=jnp.float...  58.8 us
    dot_general x2, matrix products, contract_rows(): lax.dot_general(left, right, (((0,), (0,)), ((), ())), preferred_element_...  26.1 us
    dot_general x1, matrix products, contract_cols(): lax.dot_general(left, right, (((1,), (1,)), ((), ())), preferred_element_...  12.4 us
    dot_general x1, matrix products, body(): jnp.dot(recon_grad, enc_weight, preferred_element_type=jnp.float32)  9.84 us
    convert_element_type x1, other arithmetic, body(): update = (weight_grad / jnp.sqrt(fresh)).astype(jnp.bfloat16)  9.72 us
  transfers between devices with their start and end apart: 4, of which 4 were waited for; matrix products, arithmetic and copies ran while one was open for 0% of the time, Pallas kernels for 0%

commit v1 on v0

v1 whole, which is shorter than its diff:
```python
import jax
import jax.numpy as jnp
from jax import lax
from jax.sharding import Mesh
from jax.sharding import PartitionSpec as P

D = 8192

SHARP = 4.0
SPARSITY = 2.0
BETA = 0.9

PLANE = ("xh", "y", "c", "xl")
CHIPS = ("xh", "xl", "y")
SWAP = ((0, 1), (1, 0))


def contract_rows(left, right):
    return lax.dot_general(
        left, right, (((0,), (0,)), ((), ())), preferred_element_type=jnp.float32
    )


def contract_cols(left, right):
    return lax.dot_general(
        left, right, (((1,), (1,)), ((), ())), preferred_element_type=jnp.float32
    )


def matmul(left, right):
    return jnp.dot(left, right, preferred_element_type=jnp.float32)


def bf16(a):
    return a.astype(jnp.bfloat16)


def f32(a):
    return a.astype(jnp.float32)


def shift(a, k):
    return lax.ppermute(a, "z", [(i, (i + k) % 4) for i in range(4)])


def swap(a):
    return lax.ppermute(a, "c", SWAP)


def scatter_chips(part):
    got = lax.all_to_all(part, CHIPS, 0, 0, tiled=True)
    return jnp.sum(f32(got.reshape(16, 16, -1)), axis=0)


def gather_chips(shard):
    copies = jnp.broadcast_to(shard[None], (16,) + shard.shape).reshape(256, -1)
    return lax.all_to_all(copies, CHIPS, 0, 0, tiled=True)


def scatter_rows(own, other):
    total = jnp.concatenate([f32(own[:64]), f32(other[:64])])
    for r in (2, 1, 3):
        block = slice(64 * r, 64 * r + 64)
        got = jnp.concatenate([shift(own[block], r), shift(other[block], r)])
        total = total + f32(got)
    return total


def gather_rows(shard):
    got = {r: shift(shard, -r) for r in (2, 1, 3)}
    return [shard, got[1], got[2], got[3]]


def halves(blocks):
    return jnp.concatenate([b[:64] for b in blocks] + [b[64:] for b in blocks])


def body(attn_out, out_proj, resid, enc_weight, enc_bias, dec_bias, moment):
    tokens = attn_out.shape[0]
    z = lax.axis_index("z")
    core = lax.axis_index("c")
    chip = (lax.axis_index("xh") * 2 + lax.axis_index("xl")) * 4 + lax.axis_index("y")

    def rows_of(half):
        side = jnp.where(half == 0, core, 1 - core)
        return jnp.concatenate(
            [
                lax.dynamic_slice_in_dim(attn_out, ((z + r) % 4) * 128 + side * 64, 64, 0)
                for r in range(4)
            ]
        )

    theirs = swap(bf16(matmul(rows_of(1), out_proj)))
    summed = bf16(matmul(rows_of(0), out_proj) + f32(theirs))
    first = ((z + chip // 4) % 4) * 128 + core * 64 + (chip % 4) * 16
    resid_shard = lax.dynamic_slice_in_dim(resid, first, 16, 0)
    harvested_shard = bf16(f32(resid_shard) + scatter_chips(summed))
    harvested = gather_chips(harvested_shard)
    harvested_other = swap(harvested)

    preact = (
        scatter_rows(
            bf16(matmul(harvested, enc_weight)), bf16(matmul(harvested_other, enc_weight))
        )
        + enc_bias
    )
    codes = bf16(jax.nn.softplus(SHARP * preact) / SHARP)
    slopes = jax.nn.sigmoid(SHARP * preact)
    code_blocks = gather_rows(codes)

    own_parts = []
    for block in code_blocks:
        part = contract_cols(block, enc_weight)
        own_parts.append(part[:64] + f32(swap(bf16(part[64:]))))
    recon = scatter_chips(bf16(jnp.concatenate(own_parts))) + dec_bias
    grad_shard = bf16((recon - f32(harvested_shard)) / tokens)
    recon_grad = gather_chips(grad_shard)
    recon_grad_other = swap(recon_grad)

    feedback = (
        scatter_rows(
            bf16(matmul(recon_grad, enc_weight)), bf16(matmul(recon_grad_other, enc_weight))
        )
        + SPARSITY / tokens
    )
    code_grad = halves(gather_rows(bf16(feedback * slopes)))
    weight_grad = contract_rows(
        jnp.concatenate([recon_grad, recon_grad_other]), halves(code_blocks)
    ) + contract_rows(jnp.concatenate([harvested, harvested_other]), code_grad)
    energy = jnp.sum(weight_grad * weight_grad, axis=0)
    energy = (energy + shift(energy, 2)) + (shift(energy, 1) + shift(energy, 3))
    fresh = BETA * moment + (1.0 - BETA) * (energy / D)
    update = bf16(weight_grad / jnp.sqrt(fresh))
    return (update, fresh)


def solution(mesh):
    fine = Mesh(mesh.devices.reshape(2, 4, 2, 4, 2), ("xh", "y", "c", "z", "xl"))
    placed = (
        P(None, PLANE),
        P(PLANE, "z"),
        P(None, "z"),
        P("z", PLANE),
        P(PLANE),
        P("z"),
        P(PLANE),
    )
    return jax.shard_map(
        body,
        mesh=fine,
        in_specs=placed,
        out_specs=(P("z", PLANE), P(PLANE)),
        check_vma=False,
    )
```

time: 470 us -> 274 us (0.58)
  waiting for transfers between devices: 373 us -> 132 us
  starting transfers between devices: 0.34 us -> 40.4 us
  between operations: 13.8 us -> 1.29 us
  blocking collectives: 8.55 us -> 19.5 us
  local copies, waits for them, and re-layouts: 2.72 us -> 11.7 us
    psum x4 -> x0, waiting for transfers between devices: 373 us -> none  [the longest x1 114 us: body(): lax.psum(jnp.dot(attn_out, out_proj, preferred_element_type=jnp.float32),...]
    ppermute x0 -> x28, waiting for transfers between devices: none -> 84.6 us  [the longest x21 81 us: shift(): return lax.ppermute(a, 'z', [(i, (i + k) % 4) for i in range(4)])]
    all_to_all x0 -> x3, waiting for transfers between devices: none -> 47.6 us  [the longest x2 33.6 us: scatter_chips(): got = lax.all_to_all(part, CHIPS, 0, 0, tiled=True)]
    ppermute x0 -> x28, starting transfers between devices: none -> 25.8 us  [the longest x21 24.9 us: shift(): return lax.ppermute(a, 'z', [(i, (i + k) % 4) for i in range(4)])]
    all_to_all x0 -> x1, blocking collectives: none -> 19.5 us  [gather_chips(): return lax.all_to_all(copies, CHIPS, 0, 0, tiled=True)]
    all_to_all x0 -> x3, starting transfers between devices: none -> 14.6 us  [the longest x2 10.9 us: scatter_chips(): got = lax.all_to_all(part, CHIPS, 0, 0, tiled=True)]
    psum x1 -> x0, blocking collectives: 8.55 us -> none  [body(): energy = lax.psum(jnp.sum(weight_grad * weight_grad, axis=0), 'row') / D]
    dot_general x2, matrix products: 26.1 us -> 20.5 us  [contract_rows(): lax.dot_general(left, right, (((0,), (0,)), ((), ())), preferred_element_...]
  transfers between devices with their start and end apart: 4 -> 31, of which waited for: 4 -> 20; matrix products, arithmetic and copies ran while one was open for 0% -> 14% of each run, Pallas kernels for 0% -> 0%
where the time goes in v1:
time: 274 us
  waiting for transfers between devices  132 us (48%)
  matrix products  53.8 us (20%)
  starting transfers between devices  40.4 us (15%)
  blocking collectives  19.5 us (7%)
  other arithmetic  14.7 us (5%)
  local copies, waits for them, and re-layouts  11.7 us (4%)
    ppermute x21, waiting for transfers between devices, shift(): return lax.ppermute(a, 'z', [(i, (i + k) % 4) for i in range(4)])  81 us
    all_to_all x2, waiting for transfers between devices, scatter_chips(): got = lax.all_to_all(part, CHIPS, 0, 0, tiled=True)  33.6 us
    ppermute x21, starting transfers between devices, shift(): return lax.ppermute(a, 'z', [(i, (i + k) % 4) for i in range(4)])  24.9 us
    dot_general x6, matrix products, matmul(): return jnp.dot(left, right, preferred_element_type=jnp.float32)  21.8 us
    dot_general x2, matrix products, contract_rows(): lax.dot_general(left, right, (((0,), (0,)), ((), ())), preferred_element_...  20.5 us
    all_to_all x1, blocking collectives, gather_chips(): return lax.all_to_all(copies, CHIPS, 0, 0, tiled=True)  19.5 us
    all_to_all x1, waiting for transfers between devices, gather_chips(): return lax.all_to_all(copies, CHIPS, 0, 0, tiled=True)  14 us
    convert_element_type x5, other arithmetic, bf16(): return a.astype(jnp.bfloat16)  12.5 us
  transfers between devices with their start and end apart: 31, of which 20 were waited for; matrix products, arithmetic and copies ran while one was open for 14% of the time, Pallas kernels for 0%

profile of v1, /device:TPU:0, one launch (start us, length us, event | category | flops | bytes accessed | tf_op | source)
XLA Modules:
  0.0 273.7 jit_solution(14893768533388052284)
XLA Ops:
  0.7 1.0 constant_dynamic-slice_fusion.7
  2.5 2.6 collective-permute-done
  5.2 1.4 add_convert_fusion
  6.6 7.1 %all-to-all-start = ((bf16[16,16,2048]{2,1,0:T(8,128)(2,1)}), bf16[16,16,2048]{2,1,0:T(8,128)(2,1)S(1)}, u32[]{:S(2)}, u32[]{:S(2)}) async-start(bf16[16,16,2048]{2,1,0:T(8,128)(2,1)} %bitcast), calls=%async_computation | async-start | bytes 2097152 | tf_op jit(solution)/shard_map/all_to_all | solution.py:51
  13.8 18.1 %all-to-all-done = bf16[16,16,2048]{2,1,0:T(8,128)(2,1)S(1)} async-done(((bf16[16,16,2048]{2,1,0:T(8,128)(2,1)}), bf16[16,16,2048]{2,1,0:T(8,128)(2,1)S(1)}, u32[]{:S(2)}, u32[]{:S(2)}) %all-to-all-start) | async-done | bytes 1048608 | tf_op jit(solution)/shard_map/all_to_all | solution.py:51
  32.0 0.9 add_convert_fusion.1
  33.0 19.5 %all_to_all.33 = bf16[16,16,2048]{2,1,0:T(8,128)(2,1)S(1)} all-to-all(bf16[16,16,2048]{2,1,0:T(8,128)(2,1)S(1)} %broadcast_in_dim.4), channel_id=1, replica_groups=mesh['xh'=2,'y'=4,'c'=2,'z'=4,'xl'=2] {'xh','xl','y'}, dimensions={0} | all-to-all | bytes 2097152 | tf_op jit(solution)/shard_map/all_to_all | solution.py:57
  52.5 6.2 %convolution_convert_fusion.4 = bf16[256,2048]{1,0:T(8,128)(2,1)S(1)} fusion(bf16[256,2048]{1,0:T(8,128)(2,1)S(1)} %bitcast.30, bf16[2048,2048]{1,0:T(8,128)(2,1)} %param.10), kind=kOutput, calls=%fused_computation.8 | convolution fusion | flops 2148007936 | bytes 10485760 | tf_op jit(solution)/shard_map/dot_general | solution.py:31
  58.8 4.1 %collective-permute-start.6 = (bf16[64,2048]{1,0:T(8,128)(2,1)S(1)}, bf16[64,2048]{1,0:T(8,128)(2,1)S(1)}, u32[]{:S(2)}, u32[]{:S(2)}) collective-permute-start(bf16[64,2048]{1,0:T(8,128)(2,1)S(1)} %get-tuple-element.13), channel_id=1, source_target_pairs={{0,6},{2,0},{4,2},{6,4},{1,7},{3,1},{5,3},{7,5},{8,14},{10,8},{12,... | collective-permute-start | bytes 786440 | tf_op jit(solution)/shard_map/ppermute | solution.py:43
  62.9 1.9 collective-permute-start.2
  64.8 2.4 convolution_convert_fusion.3
  67.3 1.4 collective-permute-start.7
  68.7 0.9 collective-permute-start.5
  69.7 5.5 %collective-permute-done.6 = bf16[64,2048]{1,0:T(8,128)(2,1)S(1)} collective-permute-done((bf16[64,2048]{1,0:T(8,128)(2,1)S(1)}, bf16[64,2048]{1,0:T(8,128)(2,1)S(1)}, u32[]{:S(2)}, u32[]{:S(2)}) %collective-permute-start.6) | collective-permute-done | bytes 262176 | tf_op jit(solution)/shard_map/ppermute | solution.py:43
  75.2 3.7 %collective-permute-done.4 = bf16[64,2048]{1,0:T(8,128)(2,1)S(1)} collective-permute-done((bf16[64,2048]{1,0:T(8,128)(2,1)S(1)}, bf16[64,2048]{1,0:T(8,128)(2,1)S(1)}, u32[]{:S(2)}, u32[]{:S(2)}) %collective-permute-start.4) | collective-permute-done | bytes 262176 | tf_op jit(solution)/shard_map/ppermute | solution.py:43
  78.9 6.6 %collective-permute-done.7 = bf16[64,2048]{1,0:T(8,128)(2,1)S(1)} collective-permute-done((bf16[64,2048]{1,0:T(8,128)(2,1)S(1)}, bf16[64,2048]{1,0:T(8,128)(2,1)S(1)}, u32[]{:S(2)}, u32[]{:S(2)}) %collective-permute-start.7) | collective-permute-done | bytes 262176 | tf_op jit(solution)/shard_map/ppermute | solution.py:43
  85.5 3.4 %collective-permute-done.5 = bf16[64,2048]{1,0:T(8,128)(2,1)S(1)} collective-permute-done((bf16[64,2048]{1,0:T(8,128)(2,1)S(1)}, bf16[64,2048]{1,0:T(8,128)(2,1)S(1)}, u32[]{:S(2)}, u32[]{:S(2)}) %collective-permute-start.5) | collective-permute-done | bytes 262176 | tf_op jit(solution)/shard_map/ppermute | solution.py:43
  89.0 0.7 copy-done.9
  89.8 0.9 fusion.8
  90.7 2.9 %fusion.39 = f32[128,2048]{1,0:T(8,128)S(1)} fusion(bf16[128,2048]{1,0:T(8,128)(2,1)S(1)} %fusion.8, bf16[2048,2048]{1,0:T(8,128)(2,1)S(1)} %bitcast.25), kind=kOutput, calls=%fused_computation.87 | convolution fusion | flops 1073741824 | bytes 9961472 | tf_op jit(solution)/shard_map/dot_general | solution.py:25
  94.4 1.7 collective-permute-start.13
  96.6 12.2 %collective-permute-done.9 = bf16[128,2048]{1,0:T(8,128)(2,1)S(1)} collective-permute-done((bf16[128,2048]{1,0:T(8,128)(2,1)S(1)}, bf16[128,2048]{1,0:T(8,128)(2,1)S(1)}, u32[]{:S(2)}, u32[]{:S(2)}) %collective-permute-start.9) | collective-permute-done | bytes 524320 | tf_op jit(solution)/shard_map/ppermute | solution.py:43
  108.8 2.9 %fusion.40 = f32[128,2048]{1,0:T(8,128)S(1)} fusion(bf16[128,2048]{1,0:T(8,128)(2,1)S(1)} %collective-permute-done.9, bf16[2048,2048]{1,0:T(8,128)(2,1)S(1)} %bitcast.25), kind=kOutput, calls=%fused_computation.88 | convolution fusion | flops 1073741824 | bytes 9961472 | tf_op jit(solution)/shard_map/dot_general | solution.py:25
  111.8 7.8 %collective-permute-done.11 = bf16[128,2048]{1,0:T(8,128)(2,1)S(1)} collective-permute-done((bf16[128,2048]{1,0:T(8,128)(2,1)S(1)}, bf16[128,2048]{1,0:T(8,128)(2,1)S(1)}, u32[]{:S(2)}, u32[]{:S(2)}) %collective-permute-start.11) | collective-permute-done | bytes 524320 | tf_op jit(solution)/shard_map/ppermute | solution.py:43
  119.6 2.9 %fusion.41 = f32[128,2048]{1,0:T(8,128)S(1)} fusion(bf16[128,2048]{1,0:T(8,128)(2,1)S(1)} %collective-permute-done.11, bf16[2048,2048]{1,0:T(8,128)(2,1)S(1)} %bitcast.25), kind=kOutput, calls=%fused_computation.89 | convolution fusion | flops 1073741824 | bytes 9961472 | tf_op jit(solution)/shard_map/dot_general | solution.py:25
  122.7 2.9 %fusion.42 = f32[128,2048]{1,0:T(8,128)S(1)} fusion(bf16[128,2048]{1,0:T(8,128)(2,1)S(1)} %collective-permute-done.13, bf16[2048,2048]{1,0:T(8,128)(2,1)S(1)} %bitcast.25), kind=kOutput, calls=%fused_computation.90 | convolution fusion | flops 1073741824 | bytes 9961472 | tf_op jit(solution)/shard_map/dot_general | solution.py:25
  126.3 1.0 collective-permute-done.14
  127.4 1.1 pad_maximum_fusion
  128.5 3.8 %all-to-all-start.2 = ((bf16[16,16,2048]{2,1,0:T(8,128)(2,1)}), bf16[16,16,2048]{2,1,0:T(8,128)(2,1)S(1)}, u32[]{:S(2)}, u32[]{:S(2)}) async-start(bf16[16,16,2048]{2,1,0:T(8,128)(2,1)} %bitcast.2), calls=%async_computation.2 | async-start | bytes 2097152 | tf_op jit(solution)/shard_map/all_to_all | solution.py:51
  132.3 0.7 slice_dynamic-update-slice_fusion.15
  133.0 1.7 slice_dynamic-update-slice_fusion.14
  134.6 0.7 slice_dynamic-update-slice_fusion.13
  135.4 15.5 %all-to-all-done.2 = bf16[16,16,2048]{2,1,0:T(8,128)(2,1)S(1)} async-done(((bf16[16,16,2048]{2,1,0:T(8,128)(2,1)}), bf16[16,16,2048]{2,1,0:T(8,128)(2,1)S(1)}, u32[]{:S(2)}, u32[]{:S(2)}) %all-to-all-start.2) | async-done | bytes 1048608 | tf_op jit(solution)/shard_map/all_to_all | solution.py:51
  151.1 1.1 broadcast_in_dim.5
  152.2 3.7 %all-to-all-start.3 = ((bf16[16,16,2048]{2,1,0:T(8,128)(2,1)}), bf16[16,16,2048]{2,1,0:T(8,128)(2,1)S(1)}, u32[]{:S(2)}, u32[]{:S(2)}) async-start(bf16[16,16,2048]{2,1,0:T(8,128)(2,1)} %broadcast_in_dim.5), calls=%async_computation.3 | async-start | bytes 2097152 | tf_op jit(solution)/shard_map/all_to_all | solution.py:57
  155.9 0.7 slice_dynamic-update-slice_fusion.12
  156.6 0.7 slice_dynamic-update-slice_fusion.11
  157.3 1.7 slice_dynamic-update-slice_fusion.10
  159.0 14.0 %all-to-all-done.3 = bf16[16,16,2048]{2,1,0:T(8,128)(2,1)S(1)} async-done(((bf16[16,16,2048]{2,1,0:T(8,128)(2,1)}), bf16[16,16,2048]{2,1,0:T(8,128)(2,1)S(1)}, u32[]{:S(2)}, u32[]{:S(2)}) %all-to-all-start.3) | async-done | bytes 1048608 | tf_op jit(solution)/shard_map/all_to_all | solution.py:57
  173.0 5.7 %convolution_convert_fusion.2 = bf16[256,2048]{1,0:T(8,128)(2,1)S(1)} fusion(bf16[256,2048]{1,0:T(8,128)(2,1)S(1)} %bitcast.27, bf16[2048,2048]{1,0:T(8,128)(2,1)} %param.10), kind=kOutput, calls=%fused_computation.6 | convolution fusion | flops 2148007936 | bytes 10485760 | tf_op jit(solution)/shard_map/dot_general | solution.py:31
  178.8 2.4 collective-permute-start.20
  181.2 2.6 collective-permute-start.16
  183.8 5.7 %convolution_convert_fusion.1 = bf16[256,2048]{1,0:T(8,128)(2,1)S(1)} fusion(bf16[256,2048]{1,0:T(8,128)(2,1)S(1)} %collective-permute-done.15, bf16[2048,2048]{1,0:T(8,128)(2,1)} %param.10), kind=kOutput, calls=%fused_computation.5 | convolution fusion | flops 2148007936 | bytes 10485760 | tf_op jit(solution)/shard_map/dot_general | solution.py:31
  189.7 0.8 collective-permute-start.21
  190.4 1.3 collective-permute-start.19
  191.8 1.5 collective-permute-done.20
  193.3 0.7 slice_dynamic-update-slice_fusion.9
  194.0 2.9 %collective-permute-done.18 = bf16[64,2048]{1,0:T(8,128)(2,1)S(1)} collective-permute-done((bf16[64,2048]{1,0:T(8,128)(2,1)S(1)}, bf16[64,2048]{1,0:T(8,128)(2,1)S(1)}, u32[]{:S(2)}, u32[]{:S(2)}) %collective-permute-start.18) | collective-permute-done | bytes 262176 | tf_op jit(solution)/shard_map/ppermute | solution.py:43
  196.9 7.4 %collective-permute-done.21 = bf16[64,2048]{1,0:T(8,128)(2,1)S(1)} collective-permute-done((bf16[64,2048]{1,0:T(8,128)(2,1)S(1)}, bf16[64,2048]{1,0:T(8,128)(2,1)S(1)}, u32[]{:S(2)}, u32[]{:S(2)}) %collective-permute-start.21) | collective-permute-done | bytes 262176 | tf_op jit(solution)/shard_map/ppermute | solution.py:43
  204.3 3.4 %collective-permute-done.19 = bf16[64,2048]{1,0:T(8,128)(2,1)S(1)} collective-permute-done((bf16[64,2048]{1,0:T(8,128)(2,1)S(1)}, bf16[64,2048]{1,0:T(8,128)(2,1)S(1)}, u32[]{:S(2)}, u32[]{:S(2)}) %collective-permute-start.19) | collective-permute-done | bytes 262176 | tf_op jit(solution)/shard_map/ppermute | solution.py:43
  207.7 1.0 multiply_convert_fusion
  209.1 0.7 slice_dynamic-update-slice_fusion.8
  209.8 1.7 collective-permute-start.24
  212.1 11.5 %collective-permute-done.22 = bf16[128,2048]{1,0:T(8,128)(2,1)S(1)} collective-permute-done((bf16[128,2048]{1,0:T(8,128)(2,1)S(1)}, bf16[128,2048]{1,0:T(8,128)(2,1)S(1)}, u32[]{:S(2)}, u32[]{:S(2)}) %collective-permute-start.22) | collective-permute-done | bytes 524320 | tf_op jit(solution)/shard_map/ppermute | solution.py:43
  223.7 11.0 %collective-permute-done.23 = bf16[128,2048]{1,0:T(8,128)(2,1)S(1)} collective-permute-done((bf16[128,2048]{1,0:T(8,128)(2,1)S(1)}, bf16[128,2048]{1,0:T(8,128)(2,1)S(1)}, u32[]{:S(2)}, u32[]{:S(2)}) %collective-permute-start.23) | collective-permute-done | bytes 524320 | tf_op jit(solution)/shard_map/ppermute | solution.py:43
  234.7 0.8 collective-permute-done.24
  235.7 8.2 %fusion.3 = f32[2048,2048]{1,0:T(8,128)} fusion(bf16[512,2048]{1,0:T(8,128)(2,1)S(1)} %slice_dynamic-update-slice_fusion, bf16[256,2048]{1,0:T(8,128)(2,1)S(1)} %copy-done.19, bf16[256,2048]{1,0:T(8,128)(2,1)S(1)} %bitcast.31), kind=kOutput, calls=%fused_computation.12 | convolution fusion | flops 4299161600 | bytes 20971520 | tf_op jit(solution)/shard_map/dot_general | solution.py:19
  243.9 12.3 %multiply_reduce_fusion = (f32[2048]{0:T(1024)S(1)}, f32[2048,2048]{1,0:T(8,128)}) fusion(f32[2048,2048]{1,0:T(8,128)} %fusion.3, bf16[512,2048]{1,0:T(8,128)(2,1)} %slice_dynamic-update-slice_fusion.8, bf16[256,2048]{1,0:T(8,128)(2,1)S(1)} %collective-permute-done.15, bf16[256,2048]{1,0:T(8,128)(2,1)S(1)} %bitcast.28), kind=kOutput, calls=%fused_computation.1 | convolution fusion | flops 4311742464 | bytes 37756928 | tf_op jit(solution)/shard_map/dot_general | solution.py:19
  256.1 0.7 collective-permute-start.27
  256.8 1.3 collective-permute-start.26
  258.2 2.0 collective-permute-start.25
  260.2 1.5 collective-permute-done.26
  261.7 1.6 collective-permute-done.25
  263.9 9.7 %divide_convert_fusion = bf16[2048,2048]{1,0:T(8,128)(2,1)} fusion(f32[2048,2048]{1,0:T(8,128)} %get-tuple-element.29, f32[2048]{0:T(1024)S(1)} %get-tuple-element.2), kind=kLoop, calls=%fused_computation | loop fusion | flops 8388608 | bytes 25174016 | tf_op jit(solution)/shard_map/convert_element_type | solution.py:35
  (96 shorter events, 5.9 us)
Async XLA Ops:
  0.6 1.4 copy-start
  2.4 2.7 %collective-permute-start = (bf16[256,2048]{1,0:T(8,128)(2,1)S(1)}, bf16[256,2048]{1,0:T(8,128)(2,1)S(1)}, u32[]{:S(2)}, u32[]{:S(2)}) collective-permute-start(bf16[256,2048]{1,0:T(8,128)(2,1)S(1)} %convolution_convert_fusion), channel_id=1, source_target_pairs={{0,8},{8,0},{1,9},{9,1},{2,10},{10,2},{3,11},{11,3},{4,12},{12,4},... | collective-permute-start | bytes 3145736 | tf_op jit(solution)/shard_map/ppermute | solution.py:47
  6.6 25.2 %all-to-all-start = ((bf16[16,16,2048]{2,1,0:T(8,128)(2,1)}), bf16[16,16,2048]{2,1,0:T(8,128)(2,1)S(1)}, u32[]{:S(2)}, u32[]{:S(2)}) async-start(bf16[16,16,2048]{2,1,0:T(8,128)(2,1)} %bitcast), calls=%async_computation | async-start | bytes 2097152 | tf_op jit(solution)/shard_map/all_to_all | solution.py:51
  33.0 31.8 %slice-start = ((s8[8388608]{0:T(1024)(128)(4,1)}), s8[4194304]{0:T(1024)(128)(4,1)S(1)}, s32[]{:S(2)}) async-start(s8[8388608]{0:T(1024)(128)(4,1)} %bitcast.24), calls=%async_computation.4 | async-start | bytes 8388608
  52.5 6.2 %copy-start.13 = (bf16[16,16,2048]{2,1,0:T(8,128)(2,1)}, bf16[16,16,2048]{2,1,0:T(8,128)(2,1)S(1)}, u32[]{:S(2)}) copy-start(bf16[16,16,2048]{2,1,0:T(8,128)(2,1)S(1)} %all_to_all.33) | copy-start | bytes 3145732
  52.5 12.3 %slice-start.1 = ((s8[8388608]{0:T(1024)(128)(4,1)}), s8[4194304]{0:T(1024)(128)(4,1)S(1)}, s32[]{:S(2)}) async-start(s8[8388608]{0:T(1024)(128)(4,1)} %bitcast.24), calls=%async_computation.5 | async-start | bytes 8388608
  52.5 12.3 %collective-permute-start.1 = (bf16[256,2048]{1,0:T(8,128)(2,1)S(1)}, bf16[256,2048]{1,0:T(8,128)(2,1)S(1)}, u32[]{:S(2)}, u32[]{:S(2)}) collective-permute-start(bf16[256,2048]{1,0:T(8,128)(2,1)S(1)} %bitcast.29), channel_id=1, source_target_pairs={{0,8},{8,0},{1,9},{9,1},{2,10},{10,2},{3,11},{11,3},{4,12},{12,4},... | collective-permute-start | bytes 3145736 | tf_op jit(solution)/shard_map/ppermute | solution.py:47
  58.8 16.4 %collective-permute-start.6 = (bf16[64,2048]{1,0:T(8,128)(2,1)S(1)}, bf16[64,2048]{1,0:T(8,128)(2,1)S(1)}, u32[]{:S(2)}, u32[]{:S(2)}) collective-permute-start(bf16[64,2048]{1,0:T(8,128)(2,1)S(1)} %get-tuple-element.13), channel_id=1, source_target_pairs={{0,6},{2,0},{4,2},{6,4},{1,7},{3,1},{5,3},{7,5},{8,14},{10,8},{12,... | collective-permute-start | bytes 786440 | tf_op jit(solution)/shard_map/ppermute | solution.py:43
  62.9 16.0 %collective-permute-start.4 = (bf16[64,2048]{1,0:T(8,128)(2,1)S(1)}, bf16[64,2048]{1,0:T(8,128)(2,1)S(1)}, u32[]{:S(2)}, u32[]{:S(2)}) collective-permute-start(bf16[64,2048]{1,0:T(8,128)(2,1)S(1)} %get-tuple-element.14), channel_id=1, source_target_pairs={{0,2},{2,4},{4,6},{6,0},{1,3},{3,5},{5,7},{7,1},{8,10},{10,12},{12... | collective-permute-start | bytes 786440 | tf_op jit(solution)/shard_map/ppermute | solution.py:43
  62.9 16.0 %collective-permute-start.2 = (bf16[64,2048]{1,0:T(8,128)(2,1)S(1)}, bf16[64,2048]{1,0:T(8,128)(2,1)S(1)}, u32[]{:S(2)}, u32[]{:S(2)}) collective-permute-start(bf16[64,2048]{1,0:T(8,128)(2,1)S(1)} %get-tuple-element.15), channel_id=1, source_target_pairs={{0,4},{2,6},{4,0},{6,2},{1,5},{3,7},{5,1},{7,3},{8,12},{10,14},{12... | collective-permute-start | bytes 786440 | tf_op jit(solution)/shard_map/ppermute | solution.py:43
  64.8 2.4 copy-start.18
  67.2 22.6 %copy-start.15 = (f32[2048]{0:T(1024)S(1)}, f32[2048]{0:T(1024)}, u32[]{:S(2)}) copy-start(f32[2048]{0:T(1024)} %param.11) | copy-start | bytes 24580
  67.3 18.2 %collective-permute-start.7 = (bf16[64,2048]{1,0:T(8,128)(2,1)S(1)}, bf16[64,2048]{1,0:T(8,128)(2,1)S(1)}, u32[]{:S(2)}, u32[]{:S(2)}) collective-permute-start(bf16[64,2048]{1,0:T(8,128)(2,1)S(1)} %get-tuple-element.17), channel_id=1, source_target_pairs={{0,6},{2,0},{4,2},{6,4},{1,7},{3,1},{5,3},{7,5},{8,14},{10,8},{12,... | collective-permute-start | bytes 786440 | tf_op jit(solution)/shard_map/ppermute | solution.py:43
  68.7 20.2 %collective-permute-start.5 = (bf16[64,2048]{1,0:T(8,128)(2,1)S(1)}, bf16[64,2048]{1,0:T(8,128)(2,1)S(1)}, u32[]{:S(2)}, u32[]{:S(2)}) collective-permute-start(bf16[64,2048]{1,0:T(8,128)(2,1)S(1)} %get-tuple-element.18), channel_id=1, source_target_pairs={{0,2},{2,4},{4,6},{6,0},{1,3},{3,5},{5,7},{7,1},{8,10},{10,12},{12... | collective-permute-start | bytes 786440 | tf_op jit(solution)/shard_map/ppermute | solution.py:43
  75.2 13.8 %collective-permute-start.3 = (bf16[64,2048]{1,0:T(8,128)(2,1)S(1)}, bf16[64,2048]{1,0:T(8,128)(2,1)S(1)}, u32[]{:S(2)}, u32[]{:S(2)}) collective-permute-start(bf16[64,2048]{1,0:T(8,128)(2,1)S(1)} %get-tuple-element.19), channel_id=1, source_target_pairs={{0,4},{2,6},{4,0},{6,2},{1,5},{3,7},{5,1},{7,3},{8,12},{10,14},{12... | collective-permute-start | bytes 786440 | tf_op jit(solution)/shard_map/ppermute | solution.py:43
  78.9 14.7 %copy-start.3 = (bf16[64,2048]{1,0:T(8,128)(2,1)}, bf16[64,2048]{1,0:T(8,128)(2,1)S(1)}, u32[]{:S(2)}) copy-start(bf16[64,2048]{1,0:T(8,128)(2,1)S(1)} %collective-permute-done.4) | copy-start | bytes 786436
  78.9 14.7 %copy-start.5 = (bf16[64,2048]{1,0:T(8,128)(2,1)}, bf16[64,2048]{1,0:T(8,128)(2,1)S(1)}, u32[]{:S(2)}) copy-start(bf16[64,2048]{1,0:T(8,128)(2,1)S(1)} %collective-permute-done.2) | copy-start | bytes 786436
  85.5 3.4 %copy-start.7 = (bf16[64,2048]{1,0:T(8,128)(2,1)}, bf16[64,2048]{1,0:T(8,128)(2,1)S(1)}, u32[]{:S(2)}) copy-start(bf16[64,2048]{1,0:T(8,128)(2,1)S(1)} %collective-permute-done.7) | copy-start | bytes 786436
  88.9 0.7 copy-start.9
  89.0 0.8 copy-start.11
  93.7 2.9 %collective-permute-start.8 = (bf16[64,2048]{1,0:T(8,128)(2,1)S(1)}, bf16[64,2048]{1,0:T(8,128)(2,1)S(1)}, u32[]{:S(2)}, u32[]{:S(2)}) collective-permute-start(bf16[64,2048]{1,0:T(8,128)(2,1)S(1)} %slice.239), channel_id=1, source_target_pairs={{0,8},{8,0},{1,9},{9,1},{2,10},{10,2},{3,11},{11,3},{4,12},{12,4},... | collective-permute-start | bytes 786440 | tf_op jit(solution)/shard_map/ppermute | solution.py:47
  93.8 15.0 %collective-permute-start.9 = (bf16[128,2048]{1,0:T(8,128)(2,1)S(1)}, bf16[128,2048]{1,0:T(8,128)(2,1)S(1)}, u32[]{:S(2)}, u32[]{:S(2)}) collective-permute-start(bf16[128,2048]{1,0:T(8,128)(2,1)S(1)} %fusion.8), channel_id=1, source_target_pairs={{0,6},{2,0},{4,2},{6,4},{1,7},{3,1},{5,3},{7,5},{8,14},{10,8},{12,... | collective-permute-start | bytes 1572872 | tf_op jit(solution)/shard_map/ppermute | solution.py:43
  94.4 28.3 %collective-permute-start.13 = (bf16[128,2048]{1,0:T(8,128)(2,1)S(1)}, bf16[128,2048]{1,0:T(8,128)(2,1)S(1)}, u32[]{:S(2)}, u32[]{:S(2)}) collective-permute-start(bf16[128,2048]{1,0:T(8,128)(2,1)S(1)} %fusion.8), channel_id=1, source_target_pairs={{0,2},{2,4},{4,6},{6,0},{1,3},{3,5},{5,7},{7,1},{8,10},{10,12},{12... | collective-permute-start | bytes 1572872 | tf_op jit(solution)/shard_map/ppermute | solution.py:43
  96.0 23.6 %collective-permute-start.11 = (bf16[128,2048]{1,0:T(8,128)(2,1)S(1)}, bf16[128,2048]{1,0:T(8,128)(2,1)S(1)}, u32[]{:S(2)}, u32[]{:S(2)}) collective-permute-start(bf16[128,2048]{1,0:T(8,128)(2,1)S(1)} %fusion.8), channel_id=1, source_target_pairs={{0,4},{2,6},{4,0},{6,2},{1,5},{3,7},{5,1},{7,3},{8,12},{10,14},{12... | collective-permute-start | bytes 1572872 | tf_op jit(solution)/shard_map/ppermute | solution.py:43
  108.8 2.9 %copy-start.2 = (bf16[128,2048]{1,0:T(8,128)(2,1)}, bf16[128,2048]{1,0:T(8,128)(2,1)S(1)}, u32[]{:S(2)}) copy-start(bf16[128,2048]{1,0:T(8,128)(2,1)S(1)} %collective-permute-done.9) | copy-start | bytes 1572868
  111.7 14.5 %collective-permute-start.10 = (bf16[64,2048]{1,0:T(8,128)(2,1)S(1)}, bf16[64,2048]{1,0:T(8,128)(2,1)S(1)}, u32[]{:S(2)}, u32[]{:S(2)}) collective-permute-start(bf16[64,2048]{1,0:T(8,128)(2,1)S(1)} %slice.238), channel_id=1, source_target_pairs={{0,8},{8,0},{1,9},{9,1},{2,10},{10,2},{3,11},{11,3},{4,12},{12,4},... | collective-permute-start | bytes 786440 | tf_op jit(solution)/shard_map/ppermute | solution.py:47
  122.6 3.7 %collective-permute-start.12 = (bf16[64,2048]{1,0:T(8,128)(2,1)S(1)}, bf16[64,2048]{1,0:T(8,128)(2,1)S(1)}, u32[]{:S(2)}, u32[]{:S(2)}) collective-permute-start(bf16[64,2048]{1,0:T(8,128)(2,1)S(1)} %slice.237), channel_id=1, source_target_pairs={{0,8},{8,0},{1,9},{9,1},{2,10},{10,2},{3,11},{11,3},{4,12},{12,4},... | collective-permute-start | bytes 786440 | tf_op jit(solution)/shard_map/ppermute | solution.py:47
  125.6 1.7 collective-permute-start.14
  128.5 22.6 %copy-start.16 = (f32[2048]{0:T(1024)S(1)}, f32[2048]{0:T(1024)}, u32[]{:S(2)}) copy-start(f32[2048]{0:T(1024)} %param.12) | copy-start | bytes 24580
  128.5 22.4 %all-to-all-start.2 = ((bf16[16,16,2048]{2,1,0:T(8,128)(2,1)}), bf16[16,16,2048]{2,1,0:T(8,128)(2,1)S(1)}, u32[]{:S(2)}, u32[]{:S(2)}) async-start(bf16[16,16,2048]{2,1,0:T(8,128)(2,1)} %bitcast.2), calls=%async_computation.2 | async-start | bytes 2097152 | tf_op jit(solution)/shard_map/all_to_all | solution.py:51
  152.2 20.7 %all-to-all-start.3 = ((bf16[16,16,2048]{2,1,0:T(8,128)(2,1)}), bf16[16,16,2048]{2,1,0:T(8,128)(2,1)S(1)}, u32[]{:S(2)}, u32[]{:S(2)}) async-start(bf16[16,16,2048]{2,1,0:T(8,128)(2,1)} %broadcast_in_dim.5), calls=%async_computation.3 | async-start | bytes 2097152 | tf_op jit(solution)/shard_map/all_to_all | solution.py:57
  173.0 10.8 %collective-permute-start.15 = (bf16[256,2048]{1,0:T(8,128)(2,1)S(1)}, bf16[256,2048]{1,0:T(8,128)(2,1)S(1)}, u32[]{:S(2)}, u32[]{:S(2)}) collective-permute-start(bf16[256,2048]{1,0:T(8,128)(2,1)S(1)} %bitcast.26), channel_id=1, source_target_pairs={{0,8},{8,0},{1,9},{9,1},{2,10},{10,2},{3,11},{11,3},{4,12},{12,4},... | collective-permute-start | bytes 3145736 | tf_op jit(solution)/shard_map/ppermute | solution.py:47
  178.8 14.5 %collective-permute-start.20 = (bf16[64,2048]{1,0:T(8,128)(2,1)S(1)}, bf16[64,2048]{1,0:T(8,128)(2,1)S(1)}, u32[]{:S(2)}, u32[]{:S(2)}) collective-permute-start(bf16[64,2048]{1,0:T(8,128)(2,1)S(1)} %get-tuple-element.4), channel_id=1, source_target_pairs={{0,6},{2,0},{4,2},{6,4},{1,7},{3,1},{5,3},{7,5},{8,14},{10,8},{12,... | collective-permute-start | bytes 786440 | tf_op jit(solution)/shard_map/ppermute | solution.py:43
  181.2 15.7 %collective-permute-start.18 = (bf16[64,2048]{1,0:T(8,128)(2,1)S(1)}, bf16[64,2048]{1,0:T(8,128)(2,1)S(1)}, u32[]{:S(2)}, u32[]{:S(2)}) collective-permute-start(bf16[64,2048]{1,0:T(8,128)(2,1)S(1)} %get-tuple-element.5), channel_id=1, source_target_pairs={{0,2},{2,4},{4,6},{6,0},{1,3},{3,5},{5,7},{7,1},{8,10},{10,12},{12... | collective-permute-start | bytes 786440 | tf_op jit(solution)/shard_map/ppermute | solution.py:43
  181.2 15.7 %collective-permute-start.16 = (bf16[64,2048]{1,0:T(8,128)(2,1)S(1)}, bf16[64,2048]{1,0:T(8,128)(2,1)S(1)}, u32[]{:S(2)}, u32[]{:S(2)}) collective-permute-start(bf16[64,2048]{1,0:T(8,128)(2,1)S(1)} %get-tuple-element.6), channel_id=1, source_target_pairs={{0,4},{2,6},{4,0},{6,2},{1,5},{3,7},{5,1},{7,3},{8,12},{10,14},{12... | collective-permute-start | bytes 786440 | tf_op jit(solution)/shard_map/ppermute | solution.py:43
  189.5 18.2 %copy-start.4 = (bf16[64,2048]{1,0:T(8,128)(2,1)S(1)}, bf16[64,2048]{1,0:T(8,128)(2,1)}, u32[]{:S(2)}) copy-start(bf16[64,2048]{1,0:T(8,128)(2,1)} %copy-done.3) | copy-start | bytes 786436
  189.5 18.2 %copy-start.6 = (bf16[64,2048]{1,0:T(8,128)(2,1)S(1)}, bf16[64,2048]{1,0:T(8,128)(2,1)}, u32[]{:S(2)}) copy-start(bf16[64,2048]{1,0:T(8,128)(2,1)} %copy-done.5) | copy-start | bytes 786436
  189.5 18.2 %copy-start.8 = (bf16[64,2048]{1,0:T(8,128)(2,1)S(1)}, bf16[64,2048]{1,0:T(8,128)(2,1)}, u32[]{:S(2)}) copy-start(bf16[64,2048]{1,0:T(8,128)(2,1)} %copy-done.7) | copy-start | bytes 786436
  189.5 18.2 %copy-start.10 = (bf16[64,2048]{1,0:T(8,128)(2,1)S(1)}, bf16[64,2048]{1,0:T(8,128)(2,1)}, u32[]{:S(2)}) copy-start(bf16[64,2048]{1,0:T(8,128)(2,1)} %copy-done.9) | copy-start | bytes 786436
  189.6 18.2 %copy-start.12 = (bf16[64,2048]{1,0:T(8,128)(2,1)S(1)}, bf16[64,2048]{1,0:T(8,128)(2,1)}, u32[]{:S(2)}) copy-start(bf16[64,2048]{1,0:T(8,128)(2,1)} %copy-done.11) | copy-start | bytes 786436
  189.7 14.6 %collective-permute-start.21 = (bf16[64,2048]{1,0:T(8,128)(2,1)S(1)}, bf16[64,2048]{1,0:T(8,128)(2,1)S(1)}, u32[]{:S(2)}, u32[]{:S(2)}) collective-permute-start(bf16[64,2048]{1,0:T(8,128)(2,1)S(1)} %get-tuple-element.8), channel_id=1, source_target_pairs={{0,6},{2,0},{4,2},{6,4},{1,7},{3,1},{5,3},{7,5},{8,14},{10,8},{12,... | collective-permute-start | bytes 786440 | tf_op jit(solution)/shard_map/ppermute | solution.py:43
  190.4 17.3 %collective-permute-start.19 = (bf16[64,2048]{1,0:T(8,128)(2,1)S(1)}, bf16[64,2048]{1,0:T(8,128)(2,1)S(1)}, u32[]{:S(2)}, u32[]{:S(2)}) collective-permute-start(bf16[64,2048]{1,0:T(8,128)(2,1)S(1)} %get-tuple-element.9), channel_id=1, source_target_pairs={{0,2},{2,4},{4,6},{6,0},{1,3},{3,5},{5,7},{7,1},{8,10},{10,12},{12... | collective-permute-start | bytes 786440 | tf_op jit(solution)/shard_map/ppermute | solution.py:43
  193.3 14.4 %collective-permute-start.17 = (bf16[64,2048]{1,0:T(8,128)(2,1)S(1)}, bf16[64,2048]{1,0:T(8,128)(2,1)S(1)}, u32[]{:S(2)}, u32[]{:S(2)}) collective-permute-start(bf16[64,2048]{1,0:T(8,128)(2,1)S(1)} %get-tuple-element.10), channel_id=1, source_target_pairs={{0,4},{2,6},{4,0},{6,2},{1,5},{3,7},{5,1},{7,3},{8,12},{10,14},{12... | collective-permute-start | bytes 786440 | tf_op jit(solution)/shard_map/ppermute | solution.py:43
  208.7 14.9 %collective-permute-start.22 = (bf16[128,2048]{1,0:T(8,128)(2,1)S(1)}, bf16[128,2048]{1,0:T(8,128)(2,1)S(1)}, u32[]{:S(2)}, u32[]{:S(2)}) collective-permute-start(bf16[128,2048]{1,0:T(8,128)(2,1)S(1)} %multiply_convert_fusion), channel_id=1, source_target_pairs={{0,6},{2,0},{4,2},{6,4},{1,7},{3,1},{5,3},{7,5},{8,14},{10,8},{12,... | collective-permute-start | bytes 1572872 | tf_op jit(solution)/shard_map/ppermute | solution.py:43
  209.8 25.9 %copy-start.14 = (bf16[16,16,2048]{2,1,0:T(8,128)(2,1)S(1)}, bf16[16,16,2048]{2,1,0:T(8,128)(2,1)}, u32[]{:S(2)}) copy-start(bf16[16,16,2048]{2,1,0:T(8,128)(2,1)} %copy-done.13) | copy-start | bytes 3145732
  209.8 25.9 %copy-start.19 = (bf16[256,2048]{1,0:T(8,128)(2,1)S(1)}, bf16[256,2048]{1,0:T(8,128)(2,1)}, u32[]{:S(2)}) copy-start(bf16[256,2048]{1,0:T(8,128)(2,1)} %copy-done.18) | copy-start | bytes 3145732
  209.8 25.7 %collective-permute-start.24 = (bf16[128,2048]{1,0:T(8,128)(2,1)S(1)}, bf16[128,2048]{1,0:T(8,128)(2,1)S(1)}, u32[]{:S(2)}, u32[]{:S(2)}) collective-permute-start(bf16[128,2048]{1,0:T(8,128)(2,1)S(1)} %multiply_convert_fusion), channel_id=1, source_target_pairs={{0,2},{2,4},{4,6},{6,0},{1,3},{3,5},{5,7},{7,1},{8,10},{10,12},{12... | collective-permute-start | bytes 1572872 | tf_op jit(solution)/shard_map/ppermute | solution.py:43
  211.5 23.2 %collective-permute-start.23 = (bf16[128,2048]{1,0:T(8,128)(2,1)S(1)}, bf16[128,2048]{1,0:T(8,128)(2,1)S(1)}, u32[]{:S(2)}, u32[]{:S(2)}) collective-permute-start(bf16[128,2048]{1,0:T(8,128)(2,1)S(1)} %multiply_convert_fusion), channel_id=1, source_target_pairs={{0,4},{2,6},{4,0},{6,2},{1,5},{3,7},{5,1},{7,3},{8,12},{10,14},{12... | collective-permute-start | bytes 1572872 | tf_op jit(solution)/shard_map/ppermute | solution.py:43
  243.9 19.5 %copy-start.17 = (f32[2048]{0:T(1024)S(1)}, f32[2048]{0:T(1024)}, u32[]{:S(2)}) copy-start(f32[2048]{0:T(1024)} %param.13) | copy-start | bytes 24580
  256.1 4.0 %collective-permute-start.27 = (f32[2048]{0:T(1024)S(1)}, f32[2048]{0:T(1024)S(1)}, u32[]{:S(2)}, u32[]{:S(2)}) collective-permute-start(f32[2048]{0:T(1024)S(1)} %get-tuple-element.28), channel_id=1, source_target_pairs={{0,6},{2,0},{4,2},{6,4},{1,7},{3,1},{5,3},{7,5},{8,14},{10,8},{12,... | collective-permute-start | bytes 24584 | tf_op jit(solution)/shard_map/ppermute | solution.py:43
  256.8 4.9 %collective-permute-start.26 = (f32[2048]{0:T(1024)S(1)}, f32[2048]{0:T(1024)S(1)}, u32[]{:S(2)}, u32[]{:S(2)}) collective-permute-start(f32[2048]{0:T(1024)S(1)} %get-tuple-element.28), channel_id=1, source_target_pairs={{0,2},{2,4},{4,6},{6,0},{1,3},{3,5},{5,7},{7,1},{8,10},{10,12},{12... | collective-permute-start | bytes 24584 | tf_op jit(solution)/shard_map/ppermute | solution.py:43
  258.2 5.2 %collective-permute-start.25 = (f32[2048]{0:T(1024)S(1)}, f32[2048]{0:T(1024)S(1)}, u32[]{:S(2)}, u32[]{:S(2)}) collective-permute-start(f32[2048]{0:T(1024)S(1)} %get-tuple-element.28), channel_id=1, source_target_pairs={{0,4},{2,6},{4,0},{6,2},{1,5},{3,7},{5,1},{7,3},{8,12},{10,14},{12... | collective-permute-start | bytes 24584 | tf_op jit(solution)/shard_map/ppermute | solution.py:43
  263.9 9.7 %copy-start.1 = (bf16[256,2048]{1,0:T(8,128)(2,1)S(1)}, bf16[256,2048]{1,0:T(8,128)(2,1)}, u32[]{:S(2)}) copy-start(bf16[256,2048]{1,0:T(8,128)(2,1)} %param.8) | copy-start | bytes 3145732
